TPU v7x, 128 devices: a whole 4x4x4 slice. The times are simulated.
128 devices in a mesh: patch: 64 (over x_lo, y, z, core), head: 2 (over x_hi).
Axes of the slice: x: 4 (x_hi: 2, x_lo: 2; x = x_hi * 2 + x_lo), y: 4, z: 4, core: 2. Of those that a mesh axis runs over, the one named last changes fastest.
Arguments:
- image_hidden: bfloat16 [11264, 3072], P('patch', 'head'), may hold values from -6 to 6
- mod_table: float32 [28, 3, 3072], replicated, may hold values from -3 to 3
- step_index: int32 [1], replicated, may hold values from 0 to 27
- qkv_weight: bfloat16 [3072, 3, 1536], P(None, None, 'head'), may hold values from -0.109375 to 0.109375
- norm_gain: float32 [2, 128], replicated, may hold values from 0.1 to 24
- proj_weight: bfloat16 [1536, 3072], P('head'), may hold values from -0.15625 to 0.15625
- stale_kv: bfloat16 [2, 11264, 1536], P(None, 'patch', 'head'), may hold values from -64 to 64
- text_kv: bfloat16 [2, 512, 1536], P(None, 'patch', 'head'), may hold values from -16 to 16
- patch_order: int32 [64], replicated, may hold values from 0 to 63, each once
Outputs:
- image_out: bfloat16 [11264, 3072], P('patch', 'head')
- fresh_kv: bfloat16 [2, 11264, 1536], P(None, 'patch', 'head')
Inputs may be any that keep to these rules, and one draw needn't show every extreme that they name: `patch_order`: each block index appears once.
All inputs are finite; a program needn't handle non-finite values.
Results may differ from a plain program's by a relative error of at most 0.013.
The roundings to bfloat16 on the way count: a program that leaves them out, or rounds other values in their place, can miss the bound.
Values may be sent and summed in bfloat16 or wider, within the bound.
A program may use at most 256 MiB of HBM per device.

v0:
```python
import jax
import jax.numpy as jnp
from jax import lax
from jax.sharding import PartitionSpec as P

HEAD_DIM = 128
ROW_LEN = 256


def rope_tables(positions):
    row_pos = (positions // ROW_LEN).astype(jnp.float32)
    col_pos = (positions % ROW_LEN).astype(jnp.float32)
    freq_index = jnp.arange(28, dtype=jnp.float32)
    frequency = jnp.power(jnp.float32(10000.0), -2.0 * freq_index / 56.0)
    angles = jnp.concatenate(
        [
            jnp.zeros((positions.shape[0], 8), jnp.float32),
            row_pos[:, None] * frequency[None, :],
            col_pos[:, None] * frequency[None, :],
        ],
        axis=1,
    )
    return (jnp.cos(angles), jnp.sin(angles))


def rotate(vectors, cosine, sine_part):
    pairs = vectors.reshape(vectors.shape[0], vectors.shape[1], 64, 2)
    even_part = pairs[..., 0]
    odd_part = pairs[..., 1]
    cos_rows = cosine[:, None, :]
    sin_rows = sine_part[:, None, :]
    turned = jnp.stack(
        [even_part * cos_rows - odd_part * sin_rows, even_part * sin_rows + odd_part * cos_rows],
        axis=-1,
    )
    return turned.reshape(vectors.shape)


def head_norm(vectors, gain_row):
    mean_square = jnp.mean(vectors * vectors, axis=-1, keepdims=True)
    return vectors * lax.rsqrt(mean_square + 1e-06) * gain_row


def absorb(running, queries, key_rows, value_rows, usable):
    row_max, row_sum, acc_sum = running
    head_count = queries.shape[0]
    key_count = key_rows.shape[0]
    score_scale = 1.0 / jnp.sqrt(jnp.float32(HEAD_DIM))
    for block_start in range(0, key_count, 2048):
        span_len = min(2048, key_count - block_start)
        key_part = key_rows[block_start : block_start + span_len].reshape(
            span_len, head_count, HEAD_DIM
        )
        value_part = value_rows[block_start : block_start + span_len].reshape(
            span_len, head_count, HEAD_DIM
        )
        scores = (
            jnp.einsum("htd,khd->htk", queries, key_part, preferred_element_type=jnp.float32)
            * score_scale
        )
        if usable is None:
            new_max = jnp.maximum(row_max, jnp.max(scores, axis=-1))
            exp_scores = jnp.exp(scores - new_max[..., None])
        else:
            keep = usable[block_start : block_start + span_len][None, None, :]
            new_max = jnp.maximum(row_max, jnp.max(jnp.where(keep, scores, -1e30), axis=-1))
            exp_scores = jnp.where(keep, jnp.exp(scores - new_max[..., None]), 0.0)
        shrink = jnp.exp(row_max - new_max)
        row_sum = row_sum * shrink + jnp.sum(exp_scores, axis=-1)
        acc_sum = acc_sum * shrink[..., None] + jnp.einsum(
            "htk,khd->htd",
            exp_scores.astype(jnp.bfloat16),
            value_part,
            preferred_element_type=jnp.float32,
        )
        row_max = new_max
    return (row_max, row_sum, acc_sum)


def body(
    image_hidden,
    mod_table,
    step_index,
    qkv_weight,
    norm_gain,
    proj_weight,
    stale_kv,
    text_kv,
    patch_order,
):
    whole_rows = lax.all_gather(image_hidden, "head", axis=1, tiled=True)
    tok_rows = whole_rows.shape[0]
    modulation = lax.dynamic_index_in_dim(mod_table, step_index[0], 0, keepdims=False)
    hidden = whole_rows.astype(jnp.float32)
    average = jnp.mean(hidden, axis=-1, keepdims=True)
    variance = jnp.mean((hidden - average) ** 2, axis=-1, keepdims=True)
    normed = (hidden - average) * lax.rsqrt(variance + 1e-06)
    modulated = ((1.0 + modulation[1]) * normed + modulation[0]).astype(jnp.bfloat16)
    projected_qkv = jnp.einsum(
        "td,dcf->tcf", modulated, qkv_weight, preferred_element_type=jnp.float32
    )
    feat_local = projected_qkv.shape[2]
    head_count = feat_local // HEAD_DIM
    own_index = lax.axis_index("patch")
    block_index = patch_order[own_index]
    positions = block_index * tok_rows + jnp.arange(tok_rows, dtype=jnp.int32)
    cosine, sine_part = rope_tables(positions)
    queries = rotate(
        head_norm(projected_qkv[:, 0].reshape(tok_rows, head_count, HEAD_DIM), norm_gain[0]),
        cosine,
        sine_part,
    ).astype(jnp.bfloat16)
    fresh_keys = rotate(
        head_norm(projected_qkv[:, 1].reshape(tok_rows, head_count, HEAD_DIM), norm_gain[1]),
        cosine,
        sine_part,
    ).astype(jnp.bfloat16)
    fresh_kv = jnp.stack(
        [fresh_keys.reshape(tok_rows, feat_local), projected_qkv[:, 2].astype(jnp.bfloat16)]
    )
    head_queries = queries.transpose(1, 0, 2)
    running = (
        jnp.full((head_count, tok_rows), -1e30, jnp.float32),
        jnp.zeros((head_count, tok_rows), jnp.float32),
        jnp.zeros((head_count, tok_rows, HEAD_DIM), jnp.float32),
    )
    running = absorb(running, head_queries, fresh_kv[0], fresh_kv[1], None)
    text_rows = lax.all_gather(text_kv, "patch", axis=1, tiled=True)
    running = absorb(running, head_queries, text_rows[0], text_rows[1], None)
    block_kv = lax.all_gather(stale_kv, "patch", axis=1, tiled=True)
    key_index = jnp.arange(block_kv.shape[1], dtype=jnp.int32)
    usable = key_index // tok_rows != own_index
    running = absorb(running, head_queries, block_kv[0], block_kv[1], usable)
    attended = (running[2] / running[1][..., None]).astype(jnp.bfloat16)
    attended = attended.transpose(1, 0, 2).reshape(tok_rows, feat_local)
    partial_sum = jnp.dot(attended, proj_weight, preferred_element_type=jnp.float32)
    summed = lax.psum_scatter(
        partial_sum.astype(jnp.bfloat16), "head", scatter_dimension=1, tiled=True
    ).astype(jnp.float32)
    share = summed.shape[1]
    gate_part = lax.dynamic_slice_in_dim(modulation[2], lax.axis_index("head") * share, share, 0)
    image_out = (image_hidden.astype(jnp.float32) + gate_part * summed).astype(jnp.bfloat16)
    return (image_out, fresh_kv)


def solution(mesh):
    return jax.shard_map(
        body,
        mesh=mesh,
        in_specs=(
            P("patch", "head"),
            P(),
            P(),
            P(None, None, "head"),
            P(),
            P("head", None),
            P(None, "patch", "head"),
            P(None, "patch", "head"),
            P(),
        ),
        out_specs=(P("patch", "head"), P(None, "patch", "head")),
        check_vma=False,
    )
```

profile of v0, /device:TPU:1, one launch (start us, length us, event | category | flops | bytes accessed | tf_op | source)
XLA Modules:
  0.0 687.4 jit_solution(11948454736221952406)
XLA Ops:
  17.4 21.1 %all-gather.4.cloned.1.call-done = bf16[176,3072]{1,0:T(8,128)(2,1)} async-done(((bf16[176,1536]{1,0:T(8,128)(2,1)}), bf16[176,3072]{1,0:T(8,128)(2,1)}) %all-gather.4.cloned.1.call-update) | async-done | bytes 1081360 | tf_op jit(solution)/shard_map/all_gather | solution.py:91
  41.7 8.2 %fusion.94 = f32[176,3,768]{2,0,1:T(8,128)S(1)} fusion(bf16[3072,3,768]{2,0,1:T(8,128)(2,1)} %param.12, bf16[176,3072]{1,0:T(8,128)(2,1)} %all-gather.4.cloned.1.call-done, f32[3072]{0:T(1024)S(1)} %bitcast.281, f32[176]{0:T(256)S(1)} %add_rsqrt_fusion.2, f32[176]{0:T(256)S(1)} %broadcast_multiply_fusion.2, f32[3072]{0:T(1024)S(1)} %bitcast.280), kind=kOutput, calls=%fused_computation.95 | convolution fusion | flops 2494660608 | bytes 16885120 | tf_op jit(solution)/shard_map/td,dcf->tcf/dot_general | solution.py:99
  62.0 81.1 %all-gather.6.cloned.1.call-done = bf16[2,512,768]{2,0,1:T(2,128)(2,1)} async-done(((bf16[2,8,768]{2,0,1:T(2,128)(2,1)}), bf16[2,512,768]{2,0,1:T(2,128)(2,1)}) %all-gather.6.cloned.1.call-update) | async-done | bytes 1572880 | tf_op jit(solution)/shard_map/all_gather | solution.py:128
  156.7 180.4 %all-gather.8.cloned.1.call-done = bf16[2,11264,768]{2,0,1:T(2,128)(2,1)} async-done(((bf16[2,176,768]{2,0,1:T(2,128)(2,1)}), bf16[2,11264,768]{2,0,1:T(2,128)(2,1)}) %all-gather.8.cloned.1.call-update) | async-done | bytes 34603024 | tf_op jit(solution)/shard_map/all_gather | solution.py:130
  337.1 8.7 %fusion.162 = (bf16[1,1024,768]{2,0,1:T(2,128)(2,1)S(1)}, bf16[1,1024,768]{2,0,1:T(2,128)(2,1)}) fusion(bf16[2,11264,768]{2,0,1:T(2,128)(2,1)} %all-gather.8.cloned.1.call-done), kind=kLoop, calls=%fused_computation.220 | loop fusion | bytes 6291456 | tf_op jit(solution)/shard_map/slice | solution.py:51
  345.8 8.2 %copy.148 = bf16[1,1024,768]{1,2,0:T(8,128)(2,1)} copy(bf16[1,1024,768]{2,0,1:T(2,128)(2,1)} %get-tuple-element.31) | data formatting | bytes 3145728
  354.1 6.2 copy.147
  360.3 62.9 %fusion.161 = (bf16[1,2048,768]{2,0,1:T(2,128)(2,1)}, bf16[1,2048,768]{2,0,1:T(2,128)(2,1)}, bf16[1,2048,768]{2,0,1:T(2,128)(2,1)}, bf16[1,2048,768]{2,0,1:T(2,1...) fusion(bf16[2,11264,768]{2,0,1:T(2,128)(2,1)} %all-gather.8.clo, ...), kind=kLoop, calls=%fused_computation.219 | loop fusion | bytes 62914560 | tf_op jit(solution)/shard_map/slice | solution.py:54
  423.2 15.4 %copy.145 = bf16[1,2048,768]{1,2,0:T(8,128)(2,1)} copy(bf16[1,2048,768]{2,0,1:T(2,128)(2,1)} %get-tuple-element.22) | data formatting | bytes 6291456
  438.5 15.2 %copy.143 = bf16[1,2048,768]{1,2,0:T(8,128)(2,1)} copy(bf16[1,2048,768]{2,0,1:T(2,128)(2,1)} %get-tuple-element.24) | data formatting | bytes 6291456
  453.8 15.4 %copy.141 = bf16[1,2048,768]{1,2,0:T(8,128)(2,1)} copy(bf16[1,2048,768]{2,0,1:T(2,128)(2,1)} %get-tuple-element.26) | data formatting | bytes 6291456
  469.2 15.3 %copy.139 = bf16[1,2048,768]{1,2,0:T(8,128)(2,1)} copy(bf16[1,2048,768]{2,0,1:T(2,128)(2,1)} %get-tuple-element.28) | data formatting | bytes 6291456
  484.5 13.8 %copy.137 = bf16[1,2048,768]{1,2,0:T(8,128)(2,1)S(1)} copy(bf16[1,2048,768]{2,0,1:T(2,128)(2,1)} %get-tuple-element.29) | data formatting | bytes 6291456
  500.8 5.1 select_reduce_fusion
  505.9 4.9 select_reduce_fusion.1
  510.8 5.0 select_reduce_fusion.2
  515.8 4.9 select_reduce_fusion.3
  520.8 5.0 select_reduce_fusion.4
  529.0 13.4 %copy.146 = bf16[1,2048,768]{1,2,0:T(8,128)(2,1)S(1)} copy(bf16[1,2048,768]{2,0,1:T(2,128)(2,1)} %get-tuple-element.21) | data formatting | bytes 6291456
  542.4 4.7 fusion.8
  547.1 5.9 fusion.68
  553.0 13.4 %copy.144 = bf16[1,2048,768]{1,2,0:T(8,128)(2,1)S(1)} copy(bf16[1,2048,768]{2,0,1:T(2,128)(2,1)} %get-tuple-element.23) | data formatting | bytes 6291456
  571.0 5.9 fusion.65
  576.9 13.4 %copy.142 = bf16[1,2048,768]{1,2,0:T(8,128)(2,1)S(1)} copy(bf16[1,2048,768]{2,0,1:T(2,128)(2,1)} %get-tuple-element.25) | data formatting | bytes 6291456
  594.9 5.9 fusion.62
  600.8 13.4 %copy.140 = bf16[1,2048,768]{1,2,0:T(8,128)(2,1)S(1)} copy(bf16[1,2048,768]{2,0,1:T(2,128)(2,1)} %get-tuple-element.27) | data formatting | bytes 6291456
  614.2 4.6 fusion.2
  618.7 5.9 fusion.59
  624.6 13.4 %copy.138 = bf16[1,2048,768]{1,2,0:T(8,128)(2,1)S(1)} copy(bf16[1,2048,768]{2,0,1:T(2,128)(2,1)} %get-tuple-element.20) | data formatting | bytes 6291456
  638.0 4.7 fusion
  642.8 4.8 fusion.56
  656.6 22.0 %reduce-scatter.2.cloned.1.call-done = bf16[176,1536]{1,0:T(8,128)(2,1)} async-done(((bf16[176,3072]{1,0:T(8,128)(2,1)}), bf16[176,1536]{1,0:T(8,128)(2,1)}) %reduce-scatter.2.cloned.1.call-update) | async-done | bytes 540688 | tf_op jit(solution)/shard_map/reduce_scatter | solution.py:137
  (125 shorter events, 63.1 us)
Async XLA Ops:
  7.2 31.4 %all-gather.4.cloned.1.call-start = ((), (), s32[]{:S(2)}) async-start(), calls=%async_computation.1 | async-start | bytes 1622016 | tf_op jit(solution)/shard_map/all_gather | solution.py:91
  7.9 135.2 %all-gather.6.cloned.1.call-start = ((), (), s32[]{:S(2)}) async-start(), calls=%async_computation.2 | async-start | bytes 1597440 | tf_op jit(solution)/shard_map/all_gather | solution.py:128
  9.3 327.7 %all-gather.8.cloned.1.call-start = ((), (), s32[]{:S(2)}) async-start(), calls=%async_computation.3 | async-start | bytes 35143680 | tf_op jit(solution)/shard_map/all_gather | solution.py:130
  11.7 666.9 %reduce-scatter.2.cloned.1.call-start = ((), (), s32[]{:S(2)}) async-start(), calls=%async_computation.4 | async-start | bytes 1622016 | tf_op jit(solution)/shard_map/reduce_scatter | solution.py:137
  16.4 36.3 %copy-start.14 = (f32[176,64]{0,1:T(8,128)}, f32[176,64]{0,1:T(8,128)S(1)}, u32[]{:S(2)}) copy-start(f32[176,64]{0,1:T(8,128)S(1)} %get-tuple-element.45) | copy-start | bytes 135172
  49.9 1.3 copy-start.10
  52.8 3.8 copy-start.21
  54.8 2.2 copy-start.15
  55.7 3.7 copy-start.13
  59.0 3.0 copy-start.6
  498.3 2.5 copy-start.3
  500.8 5.1 copy-start.2
  505.9 4.9 copy-start.1
  510.8 5.0 copy-start
  525.8 1.4 copy-start.11
  638.0 13.1 %slice-start = ((s8[4718592]{0:T(1024)(128)(4,1)}), s8[4194304]{0:T(1024)(128)(4,1)S(1)}, s32[]{:S(2)}) async-start(s8[4718592]{0:T(1024)(128)(4,1)} %bitcast.270), calls=%async_computation.5 | async-start | bytes 8388608
  642.7 4.9 copy-start.4
  642.8 5.7 copy-start.5
  642.8 5.9 copy-start.12
  642.8 8.4 %slice-start.1 = ((s8[4718592]{0:T(1024)(128)(4,1)}), s8[524288]{0:T(1024)(128)(4,1)S(1)}, s32[]{:S(2)}) async-start(s8[4718592]{0:T(1024)(128)(4,1)} %bitcast.270), calls=%async_computation.6 | async-start | bytes 1048576
  647.6 1.9 copy-start.8
  647.6 1.9 copy-start.16
  647.6 1.9 copy-start.17
  647.7 1.9 copy-start.18
  647.7 1.9 copy-start.19
  647.7 1.9 copy-start.20
  651.2 3.0 copy-start.7
  651.2 27.4 %copy-start.9 = (bf16[176,1536]{1,0:T(8,128)(2,1)S(1)}, bf16[176,1536]{1,0:T(8,128)(2,1)}, u32[]{:S(2)}) copy-start(bf16[176,1536]{1,0:T(8,128)(2,1)} %param.9) | copy-start | bytes 1622020
Sparse Core Ops, SparseCore 0:
  9.6 28.8 all-gather.3
  40.3 102.7 all-gather.5
  145.4 191.6 all-gather.7
  653.3 25.1 reduce-scatter.1
where the time goes:
time: 701 us; the launch traced here: 687 us
  waiting for transfers between devices  305 us (44%)
  local copies, waits for them, and re-layouts  254 us (36%)
  matrix products  74.3 us (11%)
  other arithmetic  38 us (5%)
  between operations  16 us (2%)
    all_gather x1, waiting for transfers between devices, body(): block_kv = lax.all_gather(stale_kv, 'patch', axis=1, tiled=True)  180 us
    unnamed x64, local copies, waits for them, and re-layouts  167 us
    all_gather x1, waiting for transfers between devices, body(): text_rows = lax.all_gather(text_kv, 'patch', axis=1, tiled=True)  81.1 us
    slice x1, local copies, waits for them, and re-layouts, absorb(): value_rows[block_start:block_start + span_len]  62.9 us
    dot_general x8, matrix products, absorb(): jnp.einsum('htk,khd->htd', exp_scores.astype(jnp.bfloat16), value_part, p...  32.5 us
    dot_general x8, matrix products, absorb(): jnp.einsum('htd,khd->htk', queries, key_part, preferred_element_type=jnp....  31.6 us
    reduce_sum x8, other arithmetic, absorb(): row_sum = row_sum * shrink + jnp.sum(exp_scores, axis=-1)  25.2 us
    reduce_scatter x1, waiting for transfers between devices, body(): lax.psum_scatter(partial_sum.astype(jnp.bfloat16), 'head', scatter_dimens...  22 us
  transfers between devices with their start and end apart: 4, of which 4 were waited for; matrix products, arithmetic and copies ran while one was open for 7% of the time, Pallas kernels for 0%

commit v1 on v0

v1 whole, which is shorter than its diff:
```python
import functools

import jax
import jax.numpy as jnp
import numpy as np
from jax import lax
from jax.experimental import pallas as pl
from jax.experimental.pallas import tpu as pltpu
from jax.sharding import PartitionSpec as P

MESH = pl.DeviceIdType.MESH
TOK = 176
HALF = 1536
FEAT = 768
WIDE = 384
HD = 128
KEYS = 2944
KROWS = 3296
TEXT_ROW = 2816
LOG2E = 1.4426950408889634
SCORE = LOG2E / 128.0**0.5
CHUNKS = ((0, 96), (96, 80))
NT = (((1,), (1,)), ((), ()))


def stale_row(dz, dy, s):
    if dz == 0 and dy == 0:
        return jnp.where(s == 0, 2944, 176) if not isinstance(s, int) else (2944, 176)[s]
    if dz == 0:
        return 352 + ((dy - 1) * 2 + s) * TOK
    return 352 + (6 + dy * 2 + s) * TOK


def rows_at(start, n=TOK):
    if isinstance(start, int):
        return pl.ds(start, n)
    return pl.ds(pl.multiple_of(start, 16), n)


def lanes_at(start, n):
    if isinstance(start, int):
        return pl.ds(start, n)
    return pl.ds(pl.multiple_of(start, 128), n)


def kernel(
    hidden_ref, table_ref, step_ref, wqkv_ref, gain_ref, wproj_ref, stale_ref, text_ref, order_ref, freq_ref,
    out_ref, fresh_ref,
    w, wp, table, modv, hid, modded, qs, qb, kvb, fk, tx, tf, cost, sint,
    s1, s2, ob, orx, st, strx, psend, precv, pown, outb,
    lsem, hsend, hrecv, kvsend, kvrecv, fsem, fsend, tsend, trecv, qsend, qrecv,
    osend, orecv, stsend, strecv, prsend, prrecv,
):
    p = lax.axis_index("patch")
    h = lax.axis_index("head")
    x = p // 32
    y = (p // 8) % 4
    z = (p // 2) % 4
    c = p % 2
    zp = z + 1 - 2 * (z % 2)

    def dev(xx, yy, zz, cc):
        return (xx * 32 + yy * 8 + zz * 2 + cc, h)

    def ym(d):
        return (y + d) % 4

    partner = (p, 1 - h)
    other = dev(x, y, z, 1 - c)

    def kv_dev(dz, dy, cc):
        return dev(x, ym(dy), z if dz == 0 else zp, cc)

    def q_dev(r, cc):
        return dev(1 - x if r % 2 else x, y, (z + 2) % 4 if r // 2 else z, cc)

    def remote(src, dst, ss, rs, to):
        return pltpu.make_async_remote_copy(
            src_ref=src, dst_ref=dst, send_sem=ss, recv_sem=rs, device_id=to, device_id_type=MESH
        )

    own_cols = hid.at[h]
    loads = [
        pltpu.make_async_copy(hidden_ref, own_cols, lsem.at[0]),
        pltpu.make_async_copy(table_ref, table, lsem.at[1]),
        pltpu.make_async_copy(wqkv_ref.at[0], w.at[0], lsem.at[2]),
        pltpu.make_async_copy(wqkv_ref.at[1], w.at[1], lsem.at[3]),
        pltpu.make_async_copy(wqkv_ref.at[2], w.at[2], lsem.at[4]),
        pltpu.make_async_copy(wproj_ref, wp, lsem.at[5]),
    ]
    loads[0].start()
    loads[1].start()

    barrier = pltpu.get_barrier_semaphore()
    peers = [partner, other]
    for dz in range(2):
        for dy in range(4):
            if dz or dy:
                peers += [kv_dev(dz, dy, 0), kv_dev(dz, dy, 1)]
    for r in range(1, 4):
        peers += [q_dev(r, 0), q_dev(r, 1)]
    for peer in peers:
        pl.semaphore_signal(barrier, inc=1, device_id=peer, device_id_type=MESH)
    for load in loads[2:]:
        load.start()
    pl.semaphore_wait(barrier, len(peers))

    sends = []

    def go(copy):
        copy.start()
        sends.append(copy)

    hid_copies = []
    for i, (r0, n) in enumerate(CHUNKS):
        cp = remote(
            hidden_ref.at[pl.ds(r0, n)], hid.at[h, pl.ds(r0, n)], hsend.at[i], hrecv.at[i], partner
        )
        go(cp)
        hid_copies.append(cp)

    text_local = pltpu.make_async_copy(text_ref.at[:, lanes_at(c * WIDE, WIDE)], tx.at[c], trecv.at[c])
    text_local.start()
    go(remote(text_ref.at[:, lanes_at((1 - c) * WIDE, WIDE)], tx.at[c], tsend.at[0], trecv.at[c], other))
    for dz in range(2):
        for dy in range(4):
            if dz == 0 and dy == 0:
                continue
            slot = dz * 8 + ((4 - dy) % 4) * 2 + c
            for cc in range(2):
                go(
                    remote(
                        text_ref.at[:, pl.ds(cc * WIDE, WIDE)], tx.at[slot],
                        tsend.at[dz * 8 + dy * 2 + cc], trecv.at[slot], kv_dev(dz, dy, cc),
                    )
                )

    def kv_lanes(j):
        return lanes_at(j * HD, HD)

    kv_locals = []
    for j in range(3):
        cp = pltpu.make_async_copy(
            stale_ref.at[:, :, lanes_at(c * WIDE + j * HD, HD)],
            kvb.at[:, rows_at(stale_row(0, 0, c)), kv_lanes(j)],
            kvrecv.at[c, j],
        )
        cp.start()
        go(
            remote(
                stale_ref.at[:, :, lanes_at((1 - c) * WIDE + j * HD, HD)],
                kvb.at[:, rows_at(stale_row(0, 0, c)), kv_lanes(j)],
                kvsend.at[0, j], kvrecv.at[c, j], other,
            )
        )
        k = 1
        for dz, dy in ((1, 0), (0, 1), (0, 3)):
            back = (4 - dy) % 4
            for cc in range(2):
                go(
                    remote(
                        stale_ref.at[:, :, pl.ds(cc * WIDE + j * HD, HD)],
                        kvb.at[:, rows_at(stale_row(dz, back, c)), kv_lanes(j)],
                        kvsend.at[k, j], kvrecv.at[dz * 8 + back * 2 + c, j], kv_dev(dz, dy, cc),
                    )
                )
                k += 1

    def kv_wait(dz, dy, s, j):
        ref = kvb.at[:, rows_at(stale_row(dz, dy, s)), kv_lanes(j)]
        remote(ref, ref, kvsend.at[0, 0], kvrecv.at[dz * 8 + dy * 2 + s, j], other).wait_recv()

    block = order_ref[p]
    pos = lax.broadcasted_iota(jnp.int32, (TOK, HD), 0) + block * TOK
    row_pos = (pos >> 8).astype(jnp.float32)
    col_pos = (pos & 255).astype(jnp.float32)
    angles = row_pos * freq_ref[0:1, :] + col_pos * freq_ref[1:2, :]
    lane = lax.broadcasted_iota(jnp.int32, (TOK, HD), 1)
    even = (lane & 1) == 0
    cost[...] = jnp.cos(angles)
    sine = jnp.sin(angles)
    sint[...] = jnp.where(even, -sine, sine)

    loads[1].wait()
    step = step_ref[0]
    modv[0:1, :] = table[0, pl.ds(step, 1), :]
    modv[1:2, :] = 1.0 + table[1, pl.ds(step, 1), :]
    modv[2:3, :] = table[2, pl.ds(step, 1), :]

    def forward(j):
        k = 7
        for s in range(2):
            kv_wait(1, 0, s, j)
            src = kvb.at[:, rows_at(stale_row(1, 0, s)), kv_lanes(j)]
            for dy in (1, 3, 2):
                back = (4 - dy) % 4
                go(
                    remote(
                        src, kvb.at[:, rows_at(stale_row(1, back, s)), kv_lanes(j)],
                        kvsend.at[k, j], kvrecv.at[8 + back * 2 + s, j], kv_dev(0, dy, c),
                    )
                )
                k += 1
        for s, frm, to in ((0, 3, 1), (1, 1, 3)):
            kv_wait(0, frm, s, j)
            src = kvb.at[:, rows_at(stale_row(0, frm, s)), kv_lanes(j)]
            go(
                remote(
                    src, kvb.at[:, rows_at(stale_row(0, 2, s)), kv_lanes(j)],
                    kvsend.at[k, j], kvrecv.at[4 + s, j], kv_dev(0, to, c),
                )
            )
            k += 1

    for slot in range(16):
        remote(tx.at[slot], tx.at[slot], tsend.at[0], trecv.at[slot], other).wait_recv()
    for slot in range(16):
        both = tx[slot].astype(jnp.float32)
        tf[0, slot * 8 : slot * 8 + 8, :] = both[0:8]
        tf[1, slot * 8 : slot * 8 + 8, :] = both[8:16]
    kvb[0, TEXT_ROW : TEXT_ROW + 128, :] = tf[0].astype(jnp.bfloat16)
    kvb[1, TEXT_ROW : TEXT_ROW + 128, :] = tf[1].astype(jnp.bfloat16)

    forward(0)
    forward(1)
    forward(2)

    loads[0].wait()
    for i, (r0, n) in enumerate(CHUNKS):
        hid_copies[i].wait_recv()

        def norm_rows(g, _):
            rows = pl.ds(pl.multiple_of(r0 + g * 16, 16), 16)
            a = hid[0, rows, :].astype(jnp.float32)
            b = hid[1, rows, :].astype(jnp.float32)
            mean = (jnp.sum(a, axis=1, keepdims=True) + jnp.sum(b, axis=1, keepdims=True)) * (1.0 / 3072)
            a = a - mean
            b = b - mean
            var = (jnp.sum(a * a, axis=1, keepdims=True) + jnp.sum(b * b, axis=1, keepdims=True)) * (1.0 / 3072)
            inv = lax.rsqrt(var + 1e-6)
            modded[rows, 0:HALF] = (modv[1:2, 0:HALF] * (a * inv) + modv[0:1, 0:HALF]).astype(jnp.bfloat16)
            modded[rows, HALF:] = (modv[1:2, HALF:] * (b * inv) + modv[0:1, HALF:]).astype(jnp.bfloat16)
            return 0

        lax.fori_loop(0, n // 16, norm_rows, 0)

    def head_out(v, which):
        mean_square = jnp.mean(v * v, axis=1, keepdims=True)
        v = v * lax.rsqrt(mean_square + 1e-6) * gain_ref[which : which + 1, :]
        swapped = jnp.where(even, pltpu.roll(v, 127, 1), pltpu.roll(v, 1, 1))
        return (v * cost[...] + swapped * sint[...]).astype(jnp.bfloat16)

    for part in range(3):
        loads[2 + part].wait()
        for g2 in range(3):
            cols = pl.ds(g2 * 256, 256)
            acc = jnp.dot(modded[...], w[part, :, cols], preferred_element_type=jnp.float32)
            if part == 2:
                fk[1, :, cols] = acc.astype(jnp.bfloat16)
                continue
            for i in range(2):
                g = g2 * 2 + i
                res = head_out(acc[:, i * HD : (i + 1) * HD], part)
                if part == 1:
                    fk[0, :, g * HD : (g + 1) * HD] = res
                    continue
                qs[g] = res
                cc, j = g // 3, g % 3
                for r in range(1, 4):
                    go(remote(qs.at[g], qb.at[j, 2 * r + c], qsend.at[r, g], qrecv.at[j, 2 * r + c], q_dev(r, cc)))
        if part == 0:
            q_locals = []
            for j in range(3):
                pltpu.make_async_copy(qs.at[c * 3 + j], qb.at[j, c], qrecv.at[j, c]).start()
                go(remote(qs.at[(1 - c) * 3 + j], qb.at[j, c], qsend.at[0, j], qrecv.at[j, c], other))

    fresh_row = c * 3120
    pltpu.make_async_copy(
        fk.at[:, :, lanes_at(c * WIDE, WIDE)], kvb.at[:, rows_at(fresh_row), :], fsem.at[c]
    ).start()
    go(
        remote(
            fk.at[:, :, lanes_at((1 - c) * WIDE, WIDE)], kvb.at[:, rows_at(fresh_row), :],
            fsend.at[0], fsem.at[c], other,
        )
    )
    fresh_out = pltpu.make_async_copy(fk, fresh_ref, lsem.at[6])
    fresh_out.start()

    eye_a = lax.broadcasted_iota(jnp.int32, (128, 128), 0) == lax.broadcasted_iota(jnp.int32, (128, 128), 1)

    def q_wait(j, sub):
        remote(qb.at[j, sub], qb.at[j, sub], qsend.at[0, 0], qrecv.at[j, sub], other).wait_recv()

    def kv_wait_all(j):
        for dz in range(2):
            for dy in range(4):
                for s in range(2):
                    if (dz == 1 and dy == 0) or (dz == 0 and (dy, s) in ((3, 0), (1, 1))):
                        continue
                    kv_wait(dz, dy, s, j)

    def qk(j, r, s):
        lanes = kv_lanes(j)
        if r == 0:
            for u in range(2):
                s[u * TOK : (u + 1) * TOK, :] = lax.dot_general(
                    qb[j, u], kvb[0, pl.ds(352 * u, KEYS), lanes], NT, preferred_element_type=jnp.float32
                )
        else:
            q = qb[j, pl.ds(2 * r, 2)].reshape(2 * TOK, HD)
            s[...] = lax.dot_general(
                q, kvb[0, pl.ds(176, KEYS), lanes], NT, preferred_element_type=jnp.float32
            )

    ones = jnp.ones((KEYS, HD), jnp.bfloat16)

    def pv(j, r, s):
        lanes = kv_lanes(j)
        scores = s[...]
        top = jnp.max(scores, axis=1, keepdims=True) * SCORE
        e = jnp.exp2(scores * SCORE - top).astype(jnp.bfloat16)
        if r == 0:
            accs = []
            for u in range(2):
                vals = jnp.concatenate([kvb[1, pl.ds(352 * u, KEYS), lanes], ones], axis=1)
                accs.append(jnp.dot(e[u * TOK : (u + 1) * TOK], vals, preferred_element_type=jnp.float32))
        else:
            vals = jnp.concatenate([kvb[1, pl.ds(176, KEYS), lanes], ones], axis=1)
            acc = jnp.dot(e, vals, preferred_element_type=jnp.float32)
            accs = [acc[:TOK], acc[TOK:]]
        for u in range(2):
            acc = accs[u]
            total = acc[:, HD:]
            ob[j, 2 * r + u] = (acc[:, :HD] / total).astype(jnp.bfloat16)
            level = top[u * TOK : (u + 1) * TOK] + jnp.log2(total)
            st[2 * r + u, j, 0:1, :] = jnp.sum(jnp.where(eye_a, level[:128], 0.0), axis=0, keepdims=True)
            st[2 * r + u, j, 1:2, :] = jnp.sum(jnp.where(eye_a[:48], level[128:], 0.0), axis=0, keepdims=True)

    def o_copy(j, r, u):
        g = 3 * c + j
        return remote(ob.at[j, 2 * r + u], orx.at[g, r], osend.at[j, 2 * r + u], orecv.at[g, r], q_dev(r, u))

    def o_own(j):
        g = 3 * c + j
        local = pltpu.make_async_copy(ob.at[j, c], orx.at[g, 0], orecv.at[g, 0])
        far = remote(ob.at[j, 1 - c], orx.at[g, 0], osend.at[j, 0], orecv.at[g, 0], other)
        return local, far

    for s in range(2):
        remote(
            kvb.at[:, rows_at(s * 3120), :], kvb.at[:, rows_at(s * 3120), :], fsend.at[0], fsem.at[s], other
        ).wait_recv()
    kv_wait_all(0)
    q_wait(0, 0)
    q_wait(0, 1)
    qk(0, 0, s1)

    def head_step(j, last):
        for r in range(1, 4):
            q_wait(j, 2 * r)
            q_wait(j, 2 * r + 1)
            new, old = (s2, s1) if r % 2 else (s1, s2)
            qk(j, r, new)
            pv(j, r - 1, old)
            if r == 1:
                local, far = o_own(j)
                local.start()
                far.start()
            else:
                o_copy(j, r - 1, 0).start()
                o_copy(j, r - 1, 1).start()
        if not last:
            kv_wait_all(j + 1)
            q_wait(j + 1, 0)
            q_wait(j + 1, 1)
            qk(j + 1, 0, s1)
        pv(j, 3, s2)
        o_copy(j, 3, 0).start()
        o_copy(j, 3, 1).start()

    def loop_step(j, _):
        head_step(j, False)
        return 0

    lax.fori_loop(0, 2, loop_step, 0)
    head_step(2, True)

    pltpu.make_async_copy(st.at[c], strx.at[c, 0], strecv.at[c, 0]).start()
    go(remote(st.at[1 - c], strx.at[c, 0], stsend.at[0], strecv.at[c, 0], other))
    for r in range(1, 4):
        for u in range(2):
            go(remote(st.at[2 * r + u], strx.at[c, r], stsend.at[2 * r + u], strecv.at[c, r], q_dev(r, u)))

    for cc in range(2):
        for r in range(4):
            remote(strx.at[cc, r], strx.at[cc, r], stsend.at[0], strecv.at[cc, r], other).wait_recv()
    for g in range(6):
        for r in range(4):
            remote(orx.at[g, r], orx.at[g, r], osend.at[0, 0], orecv.at[g, r], other).wait_recv()
    for g in range(6):
        levels = [strx[g // 3, r, g % 3] for r in range(4)]
        most = jnp.maximum(jnp.maximum(levels[0], levels[1]), jnp.maximum(levels[2], levels[3]))
        weights = [jnp.exp2(v - most) for v in levels]
        total = weights[0] + weights[1] + weights[2] + weights[3]
        merged_a = jnp.zeros((128, HD), jnp.float32)
        merged_b = jnp.zeros((48, HD), jnp.float32)
        for r in range(4):
            share = weights[r] / total
            col_a = jnp.sum(jnp.where(eye_a, share[0:1], 0.0), axis=1, keepdims=True)
            col_b = jnp.sum(jnp.where(eye_a[:48], share[1:2], 0.0), axis=1, keepdims=True)
            part = orx[g, r].astype(jnp.float32)
            merged_a = merged_a + part[:128] * col_a
            merged_b = merged_b + part[128:] * col_b
        modded[0:128, g * HD : (g + 1) * HD] = merged_a.astype(jnp.bfloat16)
        modded[128:176, g * HD : (g + 1) * HD] = merged_b.astype(jnp.bfloat16)

    loads[5].wait()
    pcopies = []
    for i in range(3):
        part = jnp.dot(
            modded[:, 0:FEAT], wp[:, lanes_at((1 - h) * HALF + i * 512, 512)], preferred_element_type=jnp.float32
        )
        cols = pl.ds(i * 512, 512)
        psend[:, cols] = part.astype(jnp.bfloat16)
        cp = remote(psend.at[:, cols], precv.at[:, cols], prsend.at[i], prrecv.at[i], partner)
        go(cp)
        pcopies.append(cp)
    for i in range(3):
        pown[:, i * 512 : (i + 1) * 512] = jnp.dot(
            modded[:, 0:FEAT], wp[:, lanes_at(h * HALF + i * 512, 512)], preferred_element_type=jnp.float32
        )
    out_copies = []
    for i in range(3):
        pcopies[i].wait_recv()
        cols = slice(i * 512, (i + 1) * 512)
        gate = modv[2:3, lanes_at(h * HALF + i * 512, 512)]
        summed = pown[:, cols] + precv[:, cols].astype(jnp.float32)
        outb[:, cols] = (hid[h, :, cols].astype(jnp.float32) + gate * summed).astype(jnp.bfloat16)
        cp = pltpu.make_async_copy(
            outb.at[:, pl.ds(i * 512, 512)], out_ref.at[:, pl.ds(i * 512, 512)], lsem.at[7 + i]
        )
        cp.start()
        out_copies.append(cp)

    for cp in sends:
        cp.wait_send()
    for j in range(3):
        o_own(j)[1].wait_send()
        for r in range(1, 4):
            o_copy(j, r, 0).wait_send()
            o_copy(j, r, 1).wait_send()
    fresh_out.wait()
    for cp in out_copies:
        cp.wait()


def frequencies():
    freq = np.power(10000.0, -2.0 * np.arange(28) / 56.0).astype(np.float32)
    both = np.zeros((2, 64), np.float32)
    both[0, 8:36] = freq
    both[1, 36:64] = freq
    return np.repeat(both, 2, axis=1)


def body(
    image_hidden, mod_table, step_index, qkv_weight, norm_gain, proj_weight, stale_kv, text_kv, patch_order
):
    bf, f32 = jnp.bfloat16, jnp.float32
    anywhere = pl.BlockSpec(memory_space=pl.ANY)
    vmem = pl.BlockSpec(memory_space=pltpu.VMEM)
    smem = pl.BlockSpec(memory_space=pltpu.SMEM)
    V = pltpu.VMEM
    S = pltpu.SemaphoreType.DMA
    scratch = [
        V((3, 3072, FEAT), bf),
        V((FEAT, 3072), bf),
        V((3, 28, 3072), f32),
        V((8, 3072), f32),
        V((2, TOK, HALF), bf),
        V((TOK, 3072), bf),
        V((6, TOK, HD), bf),
        V((3, 8, TOK, HD), bf),
        V((2, KROWS, WIDE), bf),
        V((2, TOK, FEAT), bf),
        V((16, 16, WIDE), bf),
        V((2, 128, WIDE), f32),
        V((TOK, HD), f32),
        V((TOK, HD), f32),
        V((2 * TOK, KEYS), f32),
        V((2 * TOK, KEYS), f32),
        V((3, 8, TOK, HD), bf),
        V((6, 4, TOK, HD), bf),
        V((8, 3, 8, 128), f32),
        V((2, 4, 3, 8, 128), f32),
        V((TOK, HALF), bf),
        V((TOK, HALF), bf),
        V((TOK, HALF), f32),
        V((TOK, HALF), bf),
        S((10,)),
        S((2,)), S((2,)),
        S((15, 3)), S((16, 3)),
        S((2,)), S((1,)),
        S((16,)), S((16,)),
        S((4, 6)), S((3, 8)),
        S((3, 8)), S((6, 4)),
        S((8,)), S((2, 4)),
        S((3,)), S((3,)),
    ]
    call = pl.pallas_call(
        kernel,
        out_shape=(
            jax.ShapeDtypeStruct((TOK, HALF), bf),
            jax.ShapeDtypeStruct((2, TOK, FEAT), bf),
        ),
        in_specs=[
            anywhere, anywhere, smem, anywhere, vmem, anywhere, anywhere, anywhere, smem, vmem,
        ],
        out_specs=(anywhere, anywhere),
        scratch_shapes=scratch,
        compiler_params=pltpu.CompilerParams(
            collective_id=0, has_side_effects=True, vmem_limit_bytes=58 * 2**20
        ),
        cost_estimate=pl.CostEstimate(flops=10**10, bytes_accessed=2 * 10**7, transcendentals=13 * 10**6),
    )
    return call(
        image_hidden,
        jnp.transpose(mod_table, (1, 0, 2)),
        step_index,
        jnp.transpose(qkv_weight, (1, 0, 2)),
        norm_gain,
        proj_weight,
        stale_kv,
        text_kv.reshape(16, FEAT),
        patch_order,
        jnp.asarray(frequencies()),
    )


def solution(mesh):
    return jax.shard_map(
        body,
        mesh=mesh,
        in_specs=(
            P("patch", "head"),
            P(),
            P(),
            P(None, None, "head"),
            P(),
            P("head", None),
            P(None, "patch", "head"),
            P(None, "patch", "head"),
            P(),
        ),
        out_specs=(P("patch", "head"), P(None, "patch", "head")),
        check_vma=False,
    )
```

time: 701 us -> 92.7 us (0.13); the launches traced: 687 us -> 92.5 us
  waiting for transfers between devices: 305 us -> 0 us
  local copies, waits for them, and re-layouts: 254 us -> 3.76 us
  Pallas kernels: 0 us -> 87.4 us
  matrix products: 74.3 us -> 0 us
  other arithmetic: 38 us -> 0 us
  between operations: 16 us -> 1.29 us
    all_gather x3 -> x0, waiting for transfers between devices: 283 us -> none  [the longest x1 180 us: body(): block_kv = lax.all_gather(stale_kv, 'patch', axis=1, tiled=True)]
    unnamed x64 -> x2, local copies, waits for them, and re-layouts: 167 us -> 3.76 us
    pallas_call x0 -> x1, Pallas kernels: none -> 87.4 us  [body(): call(image_hidden, jnp.transpose(mod_table, (1, 0, 2)), step_index, jnp.t...]
    slice x9 -> x0, local copies, waits for them, and re-layouts: 78 us -> none  [the longest x1 62.9 us: absorb(): value_rows[block_start:block_start + span_len]]
    dot_general x18 -> x0, matrix products: 74.3 us -> none  [the longest x8 32.5 us: absorb(): jnp.einsum('htk,khd->htd', exp_scores.astype(jnp.bfloat16), value_part, p...]
    reduce_sum x12 -> x0, other arithmetic: 28.8 us -> none  [the longest x8 25.2 us: absorb(): row_sum = row_sum * shrink + jnp.sum(exp_scores, axis=-1)]
    reduce_scatter x1 -> x0, waiting for transfers between devices: 22 us -> none  [body(): lax.psum_scatter(partial_sum.astype(jnp.bfloat16), 'head', scatter_dimens...]
  transfers between devices with their start and end apart: 4 -> 0, of which waited for: 4 -> 0; matrix products, arithmetic and copies ran while one was open for 7% -> 0% of each run, Pallas kernels for 0% -> 0%
where the time goes in v1:
time: 92.7 us; the launch traced here: 92.5 us
  Pallas kernels  87.4 us (94%)
  local copies, waits for them, and re-layouts  3.76 us (4%)
  between operations  1.29 us (1%)
    pallas_call x1, Pallas kernels, body(): call(image_hidden, jnp.transpose(mod_table, (1, 0, 2)), step_index, jnp.t...  87.4 us
    unnamed x2, local copies, waits for them, and re-layouts  3.76 us

profile of v1, /device:TPU:1, one launch (start us, length us, event | category | flops | bytes accessed | tf_op | source)
XLA Modules:
  0.0 92.5 jit_solution(16362071852448483328)
XLA Ops:
  1.3 87.4 %shard_map.113 = (bf16[176,1536]{1,0:T(8,128)(2,1)}, bf16[2,176,768]{2,1,0:T(8,128)(2,1)}) custom-call(bf16[176,1536]{1,0:T(8,128)(2,1)} %hidden_ref.1, f32[3,28,3072]{2,1,0:T(8,128)} %bitcast.4, s32[1]{0:T(128)S(6)} %copy.14.step_ref, bf16[3,3072,768]{2,1,0:T(8,128)(2,1)} %bitcast.3, f32[2,128]{1,0:T(2,128)} %gain_ref.1, bf16[768,3072]{1,0:T(8,128)(2,1)} %wproj_ref.1, ...), custom_call_target="tpu_custom_call" | custom-call | flops 10000000000 | bytes 20000000 | tf_op jit(solution)/shard_map/pallas_call | solution.py:526
  88.7 1.9 %copy.15 = bf16[176,1536]{1,0:T(8,128)(2,1)} copy(bf16[176,1536]{1,0:T(8,128)(2,1)} %get-tuple-element.4) | data formatting | bytes 1081344
  90.6 1.9 %copy.16 = bf16[2,176,768]{2,1,0:T(8,128)(2,1)} copy(bf16[2,176,768]{2,1,0:T(8,128)(2,1)} %get-tuple-element.5) | data formatting | bytes 1081344

commit v2 on v1

v2 whole, which is shorter than its diff:
```python
import functools

import jax
import jax.numpy as jnp
import numpy as np
from jax import lax
from jax.experimental import pallas as pl
from jax.experimental.pallas import tpu as pltpu
from jax.sharding import PartitionSpec as P

MESH = pl.DeviceIdType.MESH
TOK = 176
BLK = 192
LIVE = 184
HALF = 1536
FEAT = 768
WIDE = 384
HD = 128
KEYS = 16 * BLK
KROWS = 18 * BLK
PIECE = 96
LOG2E = 1.4426950408889634
SCORE = LOG2E / 128.0**0.5
CHUNKS = ((0, 48), (48, 48), (96, 48), (144, 32))
NT = (((1,), (1,)), ((), ()))


def stale_row(dz, dy, s):
    if dz == 0 and dy == 0:
        return jnp.where(s == 0, 16 * BLK, BLK) if not isinstance(s, int) else (16 * BLK, BLK)[s]
    if dz == 0:
        return (2 + (dy - 1) * 2 + s) * BLK
    return (8 + dy * 2 + s) * BLK


def rows_at(start, n=BLK):
    if isinstance(start, int):
        return pl.ds(start, n)
    return pl.ds(pl.multiple_of(start, 16), n)


def lanes_at(start, n):
    if isinstance(start, int):
        return pl.ds(start, n)
    return pl.ds(pl.multiple_of(start, 128), n)


def kernel(
    hidden_ref, table_ref, step_ref, wqkv_ref, gain_ref, wproj_ref, stale_ref, text_ref, order_ref, freq_ref,
    out_ref, fresh_ref,
    w, wp, wo, table, modv, hid, modded, qs, qb, kvb, stg, txs, fk, mask, cost, sint,
    s1, s2, ob, orx, att, pown, outb,
    lsem, hsend, hrecv, kvsend, kvrecv, fsem, fsend, qsend, qrecv,
    osend, orecv, wsend, wrecv, asend, arecv,
):
    p = lax.axis_index("patch")
    h = lax.axis_index("head")
    x = p // 32
    y = (p // 8) % 4
    z = (p // 2) % 4
    c = p % 2
    zk = z + 1 - 2 * (z % 2)
    zq = (z + 3 + 2 * (z % 2)) % 4

    def dev(xx, yy, zz, cc):
        return (xx * 32 + yy * 8 + zz * 2 + cc, h)

    partner = (p, 1 - h)
    other = dev(x, y, z, 1 - c)
    beside = ((1 - x) * 32 + y * 8 + z * 2 + c, 1 - h)

    def kv_dev(dz, dy, cc):
        return dev(x, (y + dy) % 4, zk if dz else z, cc)

    def q_dev(r, cc):
        return dev(1 - x if r % 2 else x, y, zq if r // 2 else z, cc)

    def remote(src, dst, ss, rs, to):
        return pltpu.make_async_remote_copy(
            src_ref=src, dst_ref=dst, send_sem=ss, recv_sem=rs, device_id=to, device_id_type=MESH
        )

    loads = [
        pltpu.make_async_copy(hidden_ref, hid.at[h], lsem.at[0]),
        pltpu.make_async_copy(table_ref, table, lsem.at[1]),
        pltpu.make_async_copy(wqkv_ref.at[0], w.at[0], lsem.at[2]),
        pltpu.make_async_copy(wqkv_ref.at[1], w.at[1], lsem.at[3]),
        pltpu.make_async_copy(wqkv_ref.at[2], w.at[2], lsem.at[4]),
        pltpu.make_async_copy(wproj_ref.at[:, lanes_at(h * HALF, HALF)], wp, lsem.at[5]),
        pltpu.make_async_copy(stale_ref, stg.at[:, pl.ds(0, TOK)], lsem.at[6]),
        pltpu.make_async_copy(text_ref, txs, lsem.at[7]),
    ]
    for i in (6, 7, 0, 1):
        loads[i].start()

    barrier = pltpu.get_barrier_semaphore()
    peers = [partner, other, beside, kv_dev(0, 2, c)]
    for dz, dy in ((1, 0), (0, 1), (0, 3)):
        peers += [kv_dev(dz, dy, 0), kv_dev(dz, dy, 1)]
    for r in range(1, 4):
        peers += [q_dev(r, 0), q_dev(r, 1)]
    for peer in peers:
        pl.semaphore_signal(barrier, inc=1, device_id=peer, device_id_type=MESH)
    for i in (2, 3, 4, 5):
        loads[i].start()

    loads[6].wait()
    loads[7].wait()
    words = txs[...].astype(jnp.float32)
    key_tail = jnp.concatenate([words[0:8], words[0:8]], axis=0).astype(jnp.bfloat16)
    value_tail = jnp.concatenate([words[8:16], jnp.zeros((8, FEAT), jnp.float32)], axis=0).astype(jnp.bfloat16)
    stg[0, TOK:BLK, :] = key_tail
    stg[1, TOK:BLK, :] = value_tail
    fk[0, TOK:BLK, :] = key_tail
    fk[1, TOK:BLK, :] = value_tail

    pl.semaphore_wait(barrier, len(peers))

    sends = []

    def go(copy):
        copy.start()
        sends.append(copy)
        return copy

    hid_copies = [
        remote(hidden_ref.at[pl.ds(r0, n)], hid.at[h, pl.ds(r0, n)], hsend.at[i], hrecv.at[i], partner)
        for i, (r0, n) in enumerate(CHUNKS)
    ]
    hid_copies[0].start()
    hid_copies[1].start()

    def hid_next(i):
        hid_copies[i - 2].wait_send()
        go(hid_copies[i])

    def kv_lanes(j):
        return pl.ds(j * HD, HD)

    def own_blocks(j):
        rows = rows_at(stale_row(0, 0, c))
        pltpu.make_async_copy(
            stg.at[:, :, lanes_at(c * WIDE + j * HD, HD)], kvb.at[:, rows, kv_lanes(j)], kvrecv.at[c, j]
        ).start()
        k = 1
        for dz, dy in ((1, 0), (0, 1), (0, 3)):
            back = (4 - dy) % 4
            for cc in range(2):
                go(
                    remote(
                        stg.at[:, :, pl.ds(cc * WIDE + j * HD, HD)],
                        kvb.at[:, rows_at(stale_row(dz, back, c)), kv_lanes(j)],
                        kvsend.at[k, j], kvrecv.at[dz * 8 + back * 2 + c, j], kv_dev(dz, dy, cc),
                    )
                )
                k += 1
        go(
            remote(
                stg.at[:, :, lanes_at((1 - c) * WIDE + j * HD, HD)], kvb.at[:, rows, kv_lanes(j)],
                kvsend.at[0, j], kvrecv.at[c, j], other,
            )
        )

    def kv_wait(dz, dy, s, j):
        ref = kvb.at[:, rows_at(stale_row(dz, dy, s)), kv_lanes(j)]
        remote(ref, ref, kvsend.at[0, 0], kvrecv.at[dz * 8 + dy * 2 + s, j], other).wait_recv()

    def forward_y(j):
        k = 7
        for s in range(2):
            kv_wait(1, 0, s, j)
            src = kvb.at[:, rows_at(stale_row(1, 0, s)), kv_lanes(j)]
            for dy in (1, 3):
                back = (4 - dy) % 4
                go(
                    remote(
                        src, kvb.at[:, rows_at(stale_row(1, back, s)), kv_lanes(j)],
                        kvsend.at[k, j], kvrecv.at[8 + back * 2 + s, j], kv_dev(0, dy, c),
                    )
                )
                k += 1
        for s, frm, to in ((0, 3, 1), (1, 1, 3)):
            kv_wait(0, frm, s, j)
            src = kvb.at[:, rows_at(stale_row(0, frm, s)), kv_lanes(j)]
            go(
                remote(
                    src, kvb.at[:, rows_at(stale_row(0, 2, s)), kv_lanes(j)],
                    kvsend.at[k, j], kvrecv.at[4 + s, j], kv_dev(0, to, c),
                )
            )
            k += 1

    def forward_z(j):
        for s in range(2):
            kv_wait(0, 2, s, j)
            go(
                remote(
                    kvb.at[:, rows_at(stale_row(0, 2, s)), kv_lanes(j)],
                    kvb.at[:, rows_at(stale_row(1, 2, s)), kv_lanes(j)],
                    kvsend.at[13 + s, j], kvrecv.at[12 + s, j], kv_dev(1, 0, c),
                )
            )

    own_blocks(0)

    block = order_ref[p]
    pos = lax.broadcasted_iota(jnp.int32, (TOK, HD), 0) + block * TOK
    row_pos = (pos >> 8).astype(jnp.float32)
    col_pos = (pos & 255).astype(jnp.float32)
    angles = row_pos * freq_ref[0:1, :] + col_pos * freq_ref[1:2, :]
    lane = lax.broadcasted_iota(jnp.int32, (TOK, HD), 1)
    even = (lane & 1) == 0
    cost[...] = jnp.cos(angles)
    sine = jnp.sin(angles)
    sint[...] = jnp.where(even, -sine, sine)

    live = lax.broadcasted_iota(jnp.int32, (BLK, HD), 0) < LIVE
    for i in range(16):
        mask[i * BLK : (i + 1) * BLK, :] = jnp.where(live, 1.0, 0.0).astype(jnp.bfloat16)

    loads[1].wait()
    step = step_ref[0]
    modv[0:1, :] = table[0, pl.ds(step, 1), :]
    modv[1:2, :] = 1.0 + table[1, pl.ds(step, 1), :]
    modv[2:3, :] = table[2, pl.ds(step, 1), :]

    loads[0].wait()

    def layer_norm(i):
        r0, n = CHUNKS[i]
        hid_copies[i].wait_recv()

        rows = pl.ds(r0, n)
        a = hid[0, rows, :].astype(jnp.float32)
        b = hid[1, rows, :].astype(jnp.float32)
        mean = (jnp.sum(a, axis=1, keepdims=True) + jnp.sum(b, axis=1, keepdims=True)) * (1.0 / 3072)
        a = a - mean
        b = b - mean
        var = (jnp.sum(a * a, axis=1, keepdims=True) + jnp.sum(b * b, axis=1, keepdims=True)) * (1.0 / 3072)
        inv = lax.rsqrt(var + 1e-6)
        modded[rows, 0:HALF] = (modv[1:2, 0:HALF] * (a * inv) + modv[0:1, 0:HALF]).astype(jnp.bfloat16)
        modded[rows, HALF:] = (modv[1:2, HALF:] * (b * inv) + modv[0:1, HALF:]).astype(jnp.bfloat16)

    forward_y(0)
    own_blocks(1)
    hid_next(2)
    layer_norm(0)
    forward_y(1)
    own_blocks(2)
    hid_next(3)
    layer_norm(1)
    layer_norm(2)
    forward_y(2)
    layer_norm(3)

    mine = pl.ds(pl.multiple_of(c * WIDE + y * PIECE, 16), PIECE)
    go(
        remote(
            wproj_ref.at[mine, lanes_at((1 - h) * HALF, HALF)], wo.at[mine], wsend.at[0], wrecv.at[y], beside
        )
    )

    def piece_wait(d):
        yy = (y + d) % 4
        ref = wo.at[pl.ds(pl.multiple_of(c * WIDE + yy * PIECE, 16), PIECE)]
        remote(ref, ref, wsend.at[0], wrecv.at[yy], other).wait_recv()

    def head_out(v, which):
        mean_square = jnp.mean(v * v, axis=1, keepdims=True)
        v = v * lax.rsqrt(mean_square + 1e-6) * gain_ref[which : which + 1, :]
        swapped = jnp.where(even, pltpu.roll(v, 127, 1), pltpu.roll(v, 1, 1))
        return (v * cost[...] + swapped * sint[...]).astype(jnp.bfloat16)

    def send_queries(j):
        for r in (1, 2, 3):
            for cc in range(2):
                g = cc * 3 + j
                go(remote(qs.at[g], qb.at[j, 2 * r + c], qsend.at[r, g], qrecv.at[j, 2 * r + c], q_dev(r, cc)))
        pltpu.make_async_copy(qs.at[c * 3 + j], qb.at[j, c], qrecv.at[j, c]).start()
        go(remote(qs.at[(1 - c) * 3 + j], qb.at[j, c], qsend.at[0, j], qrecv.at[j, c], other))

    for part in range(3):
        loads[2 + part].wait()
        for g2 in range(3):
            cols = pl.ds(g2 * 256, 256)
            acc = jnp.dot(modded[...], w[part, :, cols], preferred_element_type=jnp.float32)
            if part == 2:
                fk[1, 0:TOK, cols] = acc.astype(jnp.bfloat16)
                continue
            for i in range(2):
                g = g2 * 2 + i
                res = head_out(acc[:, i * HD : (i + 1) * HD], part)
                if part == 1:
                    fk[0, 0:TOK, g * HD : (g + 1) * HD] = res
                    continue
                qs[g] = res
        if part == 0:
            send_queries(0)
            forward_z(0)
    send_queries(1)

    fresh_row = rows_at(c * (17 * BLK))
    pltpu.make_async_copy(fk.at[:, :, lanes_at(c * WIDE, WIDE)], kvb.at[:, fresh_row, :], fsem.at[c]).start()
    go(
        remote(
            fk.at[:, :, lanes_at((1 - c) * WIDE, WIDE)], kvb.at[:, fresh_row, :], fsend.at[0], fsem.at[c], other
        )
    )
    fresh_out = pltpu.make_async_copy(fk.at[:, pl.ds(0, TOK)], fresh_ref, lsem.at[8])
    fresh_out.start()

    eye = lax.broadcasted_iota(jnp.int32, (128, 128), 0) == lax.broadcasted_iota(jnp.int32, (128, 128), 1)

    def q_wait(j, sub):
        remote(qb.at[j, sub], qb.at[j, sub], qsend.at[0, 0], qrecv.at[j, sub], other).wait_recv()

    def kv_wait_all(j):
        for dz in range(2):
            for dy in range(4):
                for s in range(2):
                    if (dz == 1 and dy == 0) or (dz == 0 and (dy == 2 or (dy, s) in ((3, 0), (1, 1)))):
                        continue
                    kv_wait(dz, dy, s, j)

    def qk(j, r, s):
        if r == 0:
            for u in range(2):
                s[u * TOK : (u + 1) * TOK, :] = lax.dot_general(
                    qb[j, u], kvb[0, pl.ds(2 * BLK * u, KEYS), kv_lanes(j)], NT,
                    preferred_element_type=jnp.float32,
                )
        else:
            q = qb[j, 2 * r : 2 * r + 2].reshape(2 * TOK, HD)
            s[...] = lax.dot_general(
                q, kvb[0, pl.ds(BLK, KEYS), kv_lanes(j)], NT, preferred_element_type=jnp.float32
            )

    def pv(j, r, s):
        scores = s[...]
        top = jnp.max(scores, axis=1, keepdims=True) * SCORE
        e = jnp.exp2(scores * SCORE - top).astype(jnp.bfloat16)
        if r == 0:
            accs = []
            for u in range(2):
                vals = jnp.concatenate([kvb[1, pl.ds(2 * BLK * u, KEYS), kv_lanes(j)], mask[...]], axis=1)
                accs.append(jnp.dot(e[u * TOK : (u + 1) * TOK], vals, preferred_element_type=jnp.float32))
        else:
            vals = jnp.concatenate([kvb[1, pl.ds(BLK, KEYS), kv_lanes(j)], mask[...]], axis=1)
            acc = jnp.dot(e, vals, preferred_element_type=jnp.float32)
            accs = [acc[:TOK], acc[TOK:]]
        for u in range(2):
            acc = accs[u]
            total = acc[:, HD:]
            ob[j, 2 * r + u, 0:TOK, :] = (acc[:, :HD] / total).astype(jnp.bfloat16)
            level = top[u * TOK : (u + 1) * TOK] + jnp.log2(total)
            la = jnp.sum(jnp.where(eye, level[:128], 0.0), axis=0, keepdims=True)
            lb = jnp.sum(jnp.where(eye[:48], level[128:], 0.0), axis=0, keepdims=True)
            rest = jnp.concatenate([la, lb], axis=0)
            terms = []
            for _ in range(3):
                term = rest.astype(jnp.bfloat16).astype(jnp.float32)
                terms.append(term)
                rest = rest - term
            terms.append(jnp.zeros((10, HD), jnp.float32))
            ob[j, 2 * r + u, TOK:BLK, :] = jnp.concatenate(terms, axis=0).astype(jnp.bfloat16)

    def o_copy(j, r, u):
        g = 3 * c + j
        return remote(ob.at[j, 2 * r + u], orx.at[g, r], osend.at[j, 2 * r + u], orecv.at[g, r], q_dev(r, u))

    def o_send(j, r):
        if r == 0:
            g = 3 * c + j
            pltpu.make_async_copy(ob.at[j, c], orx.at[g, 0], orecv.at[g, 0]).start()
            go(remote(ob.at[j, 1 - c], orx.at[g, 0], osend.at[j, 0], orecv.at[g, 0], other))
        else:
            go(o_copy(j, r, 0))
            go(o_copy(j, r, 1))

    att_copies = []

    def merge(j):
        for cc in range(2):
            for r in range(4):
                g = 3 * cc + j
                remote(orx.at[g, r], orx.at[g, r], osend.at[0, 0], orecv.at[g, r], other).wait_recv()
        for cc in range(2):
            g = 3 * cc + j
            levels = []
            for r in range(4):
                tail = orx[g, r, TOK:BLK, :].astype(jnp.float32)
                levels.append(tail[0:2] + tail[2:4] + tail[4:6])
            most = jnp.maximum(jnp.maximum(levels[0], levels[1]), jnp.maximum(levels[2], levels[3]))
            weights = [jnp.exp2(v - most) for v in levels]
            total = weights[0] + weights[1] + weights[2] + weights[3]
            merged_a = jnp.zeros((128, HD), jnp.float32)
            merged_b = jnp.zeros((48, HD), jnp.float32)
            for r in range(4):
                share = weights[r] / total
                col_a = jnp.sum(jnp.where(eye, share[0:1], 0.0), axis=1, keepdims=True)
                col_b = jnp.sum(jnp.where(eye[:48], share[1:2], 0.0), axis=1, keepdims=True)
                part = orx[g, r, 0:TOK, :].astype(jnp.float32)
                merged_a = merged_a + part[:128] * col_a
                merged_b = merged_b + part[128:] * col_b
            att[h, j, 0:128, cc * HD : (cc + 1) * HD] = merged_a.astype(jnp.bfloat16)
            att[h, j, 128:TOK, cc * HD : (cc + 1) * HD] = merged_b.astype(jnp.bfloat16)
        att_copies.append(go(remote(att.at[h, j], att.at[h, j], asend.at[j], arecv.at[j], partner)))

    for s in range(2):
        ref = kvb.at[:, pl.ds(s * 17 * BLK, BLK), :]
        remote(ref, ref, fsend.at[0], fsem.at[s], other).wait_recv()
    units = [(0, r) for r in (0, 1, 2, 3)] + [(1, r) for r in (0, 1, 2, 3)] + [(2, r) for r in (1, 2, 3, 0)]

    def score(i):
        j, r = units[i]
        if i % 4 == 0:
            kv_wait_all(j)
        q_wait(j, 2 * r)
        q_wait(j, 2 * r + 1)
        qk(j, r, s2 if i % 2 else s1)

    score(0)
    for i in range(12):
        if i < 11:
            score(i + 1)
        pv(*units[i], s2 if i % 2 else s1)
        o_send(*units[i])
        if i == 0:
            send_queries(2)
            forward_z(1)
        elif i == 3:
            forward_z(2)
            piece_wait(0)
        elif i == 5:
            for d in (1, 3, 2):
                go(remote(wo.at[mine], wo.at[mine], wsend.at[d], wrecv.at[y], kv_dev(0, d, c)))
        elif i == 6:
            merge(0)
        elif i == 10:
            merge(1)
    for d in (1, 3, 2):
        piece_wait(d)
    half = wo.at[rows_at(c * WIDE, WIDE)]
    go(remote(half, half, wsend.at[4], wrecv.at[4], other))
    merge(2)

    loads[5].wait()
    half = wo.at[rows_at((1 - c) * WIDE, WIDE)]
    remote(half, half, wsend.at[4], wrecv.at[4], other).wait_recv()

    def rows_of(weights, j, cols):
        return jnp.concatenate(
            [weights[j * HD : (j + 1) * HD, cols], weights[WIDE + j * HD : WIDE + (j + 1) * HD, cols]], axis=0
        )

    att_copies[0].wait_recv()
    att_copies[1].wait_recv()
    for i in range(3):
        cols = pl.ds(i * 512, 512)
        acc = None
        for grp, weights, count in ((h, wp, 3), (1 - h, wo, 2)):
            for j in range(count):
                term = jnp.dot(att[grp, j], rows_of(weights, j, cols), preferred_element_type=jnp.float32)
                acc = term if acc is None else acc + term
        pown[:, cols] = acc
    att_copies[2].wait_recv()
    out_copies = []
    for i in range(3):
        cols = pl.ds(i * 512, 512)
        gate = modv[2:3, lanes_at(h * HALF + i * 512, 512)]
        summed = pown[:, cols] + jnp.dot(att[1 - h, 2], rows_of(wo, 2, cols), preferred_element_type=jnp.float32)
        outb[:, cols] = (hid[h, :, cols].astype(jnp.float32) + gate * summed).astype(jnp.bfloat16)
        cp = pltpu.make_async_copy(outb.at[:, cols], out_ref.at[:, cols], lsem.at[9 + i])
        cp.start()
        out_copies.append(cp)

    for cp in sends:
        cp.wait_send()
    fresh_out.wait()
    for cp in out_copies:
        cp.wait()


def copy_kernel(a_ref, b_ref, c_ref, d_ref, a, b, sem):
    pairs = [
        (a_ref.at[pl.ds(r, n)], a.at[pl.ds(r, n)], c_ref.at[pl.ds(r, n)]) for r, n in ((0, 96), (96, 80))
    ]
    pairs += [(b_ref.at[i], b.at[i], d_ref.at[i]) for i in range(2)]
    ins = [pltpu.make_async_copy(src, mid, sem.at[i]) for i, (src, mid, _) in enumerate(pairs)]
    outs = [pltpu.make_async_copy(mid, dst, sem.at[4 + i]) for i, (_, mid, dst) in enumerate(pairs)]
    for cp in ins:
        cp.start()
    for cp_in, cp_out in zip(ins, outs):
        cp_in.wait()
        cp_out.start()
    for cp in outs:
        cp.wait()


def frequencies():
    freq = np.power(10000.0, -2.0 * np.arange(28) / 56.0).astype(np.float32)
    both = np.zeros((2, 64), np.float32)
    both[0, 8:36] = freq
    both[1, 36:64] = freq
    return np.repeat(both, 2, axis=1)


def body(
    image_hidden, mod_table, step_index, qkv_weight, norm_gain, proj_weight, stale_kv, text_kv, patch_order
):
    bf, f32 = jnp.bfloat16, jnp.float32
    anywhere = pl.BlockSpec(memory_space=pl.ANY)
    vmem = pl.BlockSpec(memory_space=pltpu.VMEM)
    smem = pl.BlockSpec(memory_space=pltpu.SMEM)
    V = pltpu.VMEM
    S = pltpu.SemaphoreType.DMA
    scratch = [
        V((3, 3072, FEAT), bf),
        V((FEAT, HALF), bf),
        V((FEAT, HALF), bf),
        V((3, 28, 3072), f32),
        V((8, 3072), f32),
        V((2, TOK, HALF), bf),
        V((TOK, 3072), bf),
        V((6, TOK, HD), bf),
        V((3, 8, TOK, HD), bf),
        V((2, KROWS, WIDE), bf),
        V((2, BLK, FEAT), bf),
        V((16, FEAT), bf),
        V((2, BLK, FEAT), bf),
        V((KEYS, HD), bf),
        V((TOK, HD), f32),
        V((TOK, HD), f32),
        V((2 * TOK, KEYS), f32),
        V((2 * TOK, KEYS), f32),
        V((3, 8, BLK, HD), bf),
        V((6, 4, BLK, HD), bf),
        V((2, 3, TOK, 2 * HD), bf),
        V((TOK, HALF), f32),
        V((TOK, HALF), bf),
        S((12,)),
        S((4,)), S((4,)),
        S((15, 3)), S((16, 3)),
        S((2,)), S((1,)),
        S((4, 6)), S((3, 8)),
        S((3, 8)), S((6, 4)),
        S((5,)), S((5,)),
        S((3,)), S((3,)),
    ]
    call = pl.pallas_call(
        kernel,
        out_shape=(
            jax.ShapeDtypeStruct((TOK, HALF), bf),
            jax.ShapeDtypeStruct((2, TOK, FEAT), bf),
        ),
        in_specs=[
            anywhere, anywhere, smem, anywhere, vmem, anywhere, anywhere, anywhere, smem, vmem,
        ],
        out_specs=(anywhere, anywhere),
        scratch_shapes=scratch,
        compiler_params=pltpu.CompilerParams(
            collective_id=0, has_side_effects=True, vmem_limit_bytes=58 * 2**20
        ),
        cost_estimate=pl.CostEstimate(flops=10**10, bytes_accessed=2 * 10**7, transcendentals=13 * 10**6),
    )
    image_out, fresh_kv = call(
        image_hidden,
        jnp.transpose(mod_table, (1, 0, 2)),
        step_index,
        jnp.transpose(qkv_weight, (1, 0, 2)),
        norm_gain,
        proj_weight,
        stale_kv,
        text_kv.reshape(16, FEAT),
        patch_order,
        jnp.asarray(frequencies()),
    )
    return pl.pallas_call(
        copy_kernel,
        out_shape=(
            jax.ShapeDtypeStruct((TOK, HALF), bf),
            jax.ShapeDtypeStruct((2, TOK, FEAT), bf),
        ),
        in_specs=[anywhere, anywhere],
        out_specs=(anywhere, anywhere),
        scratch_shapes=[V((TOK, HALF), bf), V((2, TOK, FEAT), bf), S((8,))],
        compiler_params=pltpu.CompilerParams(vmem_limit_bytes=58 * 2**20),
    )(image_out, fresh_kv)


def solution(mesh):
    return jax.shard_map(
        body,
        mesh=mesh,
        in_specs=(
            P("patch", "head"),
            P(),
            P(),
            P(None, None, "head"),
            P(),
            P("head", None),
            P(None, "patch", "head"),
            P(None, "patch", "head"),
            P(),
        ),
        out_specs=(P("patch", "head"), P(None, "patch", "head")),
        check_vma=False,
    )
```

time: 92.7 us -> 83.9 us (0.905); the launches traced: 92.5 us -> 82.6 us
  Pallas kernels: 87.4 us -> 81.2 us
  local copies, waits for them, and re-layouts: 3.76 us -> 0 us
    pallas_call x1, Pallas kernels: 87.4 us -> 79.1 us  [body(): call(image_hidden, jnp.transpose(mod_table, (1, 0, 2)), step_index, jnp.t...]
    unnamed x2 -> x0, local copies, waits for them, and re-layouts: 3.76 us -> none
    pallas_call x0 -> x1, Pallas kernels: none -> 2.02 us  [body(): pl.pallas_call(copy_kernel, out_shape=(jax.ShapeDtypeStruct((TOK, HALF),...]
where the time goes in v2:
time: 83.9 us; the launch traced here: 82.6 us
  Pallas kernels  81.2 us (97%)
  between operations  1.47 us (2%)
    pallas_call x1, Pallas kernels, body(): call(image_hidden, jnp.transpose(mod_table, (1, 0, 2)), step_index, jnp.t...  79.1 us
    pallas_call x1, Pallas kernels, body(): pl.pallas_call(copy_kernel, out_shape=(jax.ShapeDtypeStruct((TOK, HALF),...  2.02 us

profile of v2, /device:TPU:1, one launch (start us, length us, event | category | flops | bytes accessed | tf_op | source)
XLA Modules:
  0.0 82.6 jit_solution(1531207947111183483)
XLA Ops:
  1.3 79.1 %shard_map.113 = (bf16[176,1536]{1,0:T(8,128)(2,1)}, bf16[2,176,768]{2,1,0:T(8,128)(2,1)}) custom-call(bf16[176,1536]{1,0:T(8,128)(2,1)} %hidden_ref.1, f32[3,28,3072]{2,1,0:T(8,128)} %bitcast.4, s32[1]{0:T(128)S(6)} %copy.12.step_ref, bf16[3,3072,768]{2,1,0:T(8,128)(2,1)} %bitcast.3, f32[2,128]{1,0:T(2,128)} %gain_ref.1, bf16[768,3072]{1,0:T(8,128)(2,1)} %wproj_ref.1, ...), custom_call_target="tpu_custom_call" | custom-call | flops 10000000000 | bytes 20000000 | tf_op jit(solution)/shard_map/pallas_call | solution.py:566
  80.4 2.0 %shard_map.114 = (bf16[176,1536]{1,0:T(8,128)(2,1)}, bf16[2,176,768]{2,1,0:T(8,128)(2,1)}) custom-call(bf16[176,1536]{1,0:T(8,128)(2,1)} %get-tuple-element.4.a_ref, bf16[2,176,768]{2,1,0:T(8,128)(2,1)} %get-tuple-element.5.b_ref), custom_call_target="tpu_custom_call" | custom-call | tf_op jit(solution)/shard_map/pallas_call | solution.py:578

commit v3 on v2

--- a/solution.py
+++ b/solution.py
@@ -101,8 +101,6 @@
         peers += [q_dev(r, 0), q_dev(r, 1)]
     for peer in peers:
         pl.semaphore_signal(barrier, inc=1, device_id=peer, device_id_type=MESH)
-    for i in (2, 3, 4, 5):
-        loads[i].start()
 
     loads[6].wait()
     loads[7].wait()
@@ -124,15 +122,9 @@
         return copy
 
     hid_copies = [
-        remote(hidden_ref.at[pl.ds(r0, n)], hid.at[h, pl.ds(r0, n)], hsend.at[i], hrecv.at[i], partner)
+        go(remote(hidden_ref.at[pl.ds(r0, n)], hid.at[h, pl.ds(r0, n)], hsend.at[i], hrecv.at[i], partner))
         for i, (r0, n) in enumerate(CHUNKS)
     ]
-    hid_copies[0].start()
-    hid_copies[1].start()
-
-    def hid_next(i):
-        hid_copies[i - 2].wait_send()
-        go(hid_copies[i])
 
     def kv_lanes(j):
         return pl.ds(j * HD, HD)
@@ -165,7 +157,7 @@
         ref = kvb.at[:, rows_at(stale_row(dz, dy, s)), kv_lanes(j)]
         remote(ref, ref, kvsend.at[0, 0], kvrecv.at[dz * 8 + dy * 2 + s, j], other).wait_recv()
 
-    def forward_y(j):
+    def forward_plane(j):
         k = 7
         for s in range(2):
             kv_wait(1, 0, s, j)
@@ -179,6 +171,9 @@
                     )
                 )
                 k += 1
+
+    def forward_far(j):
+        k = 11
         for s, frm, to in ((0, 3, 1), (1, 1, 3)):
             kv_wait(0, frm, s, j)
             src = kvb.at[:, rows_at(stale_row(0, frm, s)), kv_lanes(j)]
@@ -201,7 +196,10 @@
                 )
             )
 
-    own_blocks(0)
+    for j in range(3):
+        own_blocks(j)
+    for i in (2, 3, 4, 5):
+        loads[i].start()
 
     block = order_ref[p]
     pos = lax.broadcasted_iota(jnp.int32, (TOK, HD), 0) + block * TOK
@@ -241,17 +239,10 @@
         modded[rows, 0:HALF] = (modv[1:2, 0:HALF] * (a * inv) + modv[0:1, 0:HALF]).astype(jnp.bfloat16)
         modded[rows, HALF:] = (modv[1:2, HALF:] * (b * inv) + modv[0:1, HALF:]).astype(jnp.bfloat16)
 
-    forward_y(0)
-    own_blocks(1)
-    hid_next(2)
-    layer_norm(0)
-    forward_y(1)
-    own_blocks(2)
-    hid_next(3)
-    layer_norm(1)
-    layer_norm(2)
-    forward_y(2)
-    layer_norm(3)
+    for i in range(4):
+        layer_norm(i)
+    forward_far(0)
+    forward_plane(0)
 
     mine = pl.ds(pl.multiple_of(c * WIDE + y * PIECE, 16), PIECE)
     go(
@@ -296,8 +287,8 @@
                 qs[g] = res
         if part == 0:
             send_queries(0)
-            forward_z(0)
-    send_queries(1)
+            forward_far(1)
+            forward_far(2)
 
     fresh_row = rows_at(c * (17 * BLK))
     pltpu.make_async_copy(fk.at[:, :, lanes_at(c * WIDE, WIDE)], kvb.at[:, fresh_row, :], fsem.at[c]).start()
@@ -308,6 +299,10 @@
     )
     fresh_out = pltpu.make_async_copy(fk.at[:, pl.ds(0, TOK)], fresh_ref, lsem.at[8])
     fresh_out.start()
+    send_queries(1)
+    forward_plane(1)
+    forward_z(0)
+    forward_plane(2)
 
     eye = lax.broadcasted_iota(jnp.int32, (128, 128), 0) == lax.broadcasted_iota(jnp.int32, (128, 128), 1)
 
@@ -428,41 +423,43 @@
         if i == 0:
             send_queries(2)
             forward_z(1)
-        elif i == 3:
+        elif i == 1:
             forward_z(2)
+        elif i == 4:
             piece_wait(0)
-        elif i == 5:
             for d in (1, 3, 2):
                 go(remote(wo.at[mine], wo.at[mine], wsend.at[d], wrecv.at[y], kv_dev(0, d, c)))
         elif i == 6:
             merge(0)
         elif i == 10:
             merge(1)
+    def rows_of(weights, j, cols):
+        return jnp.concatenate(
+            [weights[j * HD : (j + 1) * HD, cols], weights[WIDE + j * HD : WIDE + (j + 1) * HD, cols]], axis=0
+        )
+
+    def project(pairs, first):
+        for i in range(3):
+            cols = pl.ds(i * 512, 512)
+            acc = None if first else pown[:, cols]
+            for grp, weights, j in pairs:
+                term = jnp.dot(att[grp, j], rows_of(weights, j, cols), preferred_element_type=jnp.float32)
+                acc = term if acc is None else acc + term
+            pown[:, cols] = acc
+
     for d in (1, 3, 2):
         piece_wait(d)
     half = wo.at[rows_at(c * WIDE, WIDE)]
     go(remote(half, half, wsend.at[4], wrecv.at[4], other))
+
+    loads[5].wait()
+    project([(h, wp, 0), (h, wp, 1)], True)
     merge(2)
-
-    loads[5].wait()
     half = wo.at[rows_at((1 - c) * WIDE, WIDE)]
     remote(half, half, wsend.at[4], wrecv.at[4], other).wait_recv()
-
-    def rows_of(weights, j, cols):
-        return jnp.concatenate(
-            [weights[j * HD : (j + 1) * HD, cols], weights[WIDE + j * HD : WIDE + (j + 1) * HD, cols]], axis=0
-        )
-
     att_copies[0].wait_recv()
     att_copies[1].wait_recv()
-    for i in range(3):
-        cols = pl.ds(i * 512, 512)
-        acc = None
-        for grp, weights, count in ((h, wp, 3), (1 - h, wo, 2)):
-            for j in range(count):
-                term = jnp.dot(att[grp, j], rows_of(weights, j, cols), preferred_element_type=jnp.float32)
-                acc = term if acc is None else acc + term
-        pown[:, cols] = acc
+    project([(h, wp, 2), (1 - h, wo, 0), (1 - h, wo, 1)], False)
     att_copies[2].wait_recv()
     out_copies = []
     for i in range(3):

time: 83.9 us -> 73.8 us (0.88); the launches traced: 82.6 us -> 73.6 us
  Pallas kernels: 81.2 us -> 72.1 us
    pallas_call x1, Pallas kernels: 79.1 us -> 70.1 us  [body(): call(image_hidden, jnp.transpose(mod_table, (1, 0, 2)), step_index, jnp.t...]
where the time goes in v3:
time: 73.8 us; the launch traced here: 73.6 us
  Pallas kernels  72.1 us (98%)
  between operations  1.47 us (2%)
    pallas_call x1, Pallas kernels, body(): call(image_hidden, jnp.transpose(mod_table, (1, 0, 2)), step_index, jnp.t...  70.1 us
    pallas_call x1, Pallas kernels, body(): pl.pallas_call(copy_kernel, out_shape=(jax.ShapeDtypeStruct((TOK, HALF),...  2.02 us

profile of v3, /device:TPU:1, one launch (start us, length us, event | category | flops | bytes accessed | tf_op | source)
XLA Modules:
  0.0 73.6 jit_solution(13004641572844120080)
XLA Ops:
  1.3 70.1 %shard_map.113 = (bf16[176,1536]{1,0:T(8,128)(2,1)}, bf16[2,176,768]{2,1,0:T(8,128)(2,1)}) custom-call(bf16[176,1536]{1,0:T(8,128)(2,1)} %hidden_ref.1, f32[3,28,3072]{2,1,0:T(8,128)} %bitcast.4, s32[1]{0:T(128)S(6)} %copy.12.step_ref, bf16[3,3072,768]{2,1,0:T(8,128)(2,1)} %bitcast.3, f32[2,128]{1,0:T(2,128)} %gain_ref.1, bf16[768,3072]{1,0:T(8,128)(2,1)} %wproj_ref.1, ...), custom_call_target="tpu_custom_call" | custom-call | flops 10000000000 | bytes 20000000 | tf_op jit(solution)/shard_map/pallas_call | solution.py:563
  71.4 2.0 %shard_map.114 = (bf16[176,1536]{1,0:T(8,128)(2,1)}, bf16[2,176,768]{2,1,0:T(8,128)(2,1)}) custom-call(bf16[176,1536]{1,0:T(8,128)(2,1)} %get-tuple-element.4.a_ref, bf16[2,176,768]{2,1,0:T(8,128)(2,1)} %get-tuple-element.5.b_ref), custom_call_target="tpu_custom_call" | custom-call | tf_op jit(solution)/shard_map/pallas_call | solution.py:575

commit v4 on v3

--- a/solution.py
+++ b/solution.py
@@ -18,7 +18,7 @@
 HD = 128
 KEYS = 16 * BLK
 KROWS = 18 * BLK
-PIECE = 96
+PIECE = 192
 LOG2E = 1.4426950408889634
 SCORE = LOG2E / 128.0**0.5
 CHUNKS = ((0, 48), (48, 48), (96, 48), (144, 32))
@@ -94,13 +94,27 @@
         loads[i].start()
 
     barrier = pltpu.get_barrier_semaphore()
-    peers = [partner, other, beside, kv_dev(0, 2, c)]
+    peers = [partner, other, beside]
     for dz, dy in ((1, 0), (0, 1), (0, 3)):
         peers += [kv_dev(dz, dy, 0), kv_dev(dz, dy, 1)]
     for r in range(1, 4):
         peers += [q_dev(r, 0), q_dev(r, 1)]
     for peer in peers:
         pl.semaphore_signal(barrier, inc=1, device_id=peer, device_id_type=MESH)
+
+    pl.semaphore_wait(barrier, len(peers))
+
+    sends = []
+
+    def go(copy):
+        copy.start()
+        sends.append(copy)
+        return copy
+
+    hid_copies = [
+        go(remote(hidden_ref.at[pl.ds(r0, n)], hid.at[h, pl.ds(r0, n)], hsend.at[i], hrecv.at[i], partner))
+        for i, (r0, n) in enumerate(CHUNKS)
+    ]
 
     loads[6].wait()
     loads[7].wait()
@@ -111,20 +125,6 @@
     stg[1, TOK:BLK, :] = value_tail
     fk[0, TOK:BLK, :] = key_tail
     fk[1, TOK:BLK, :] = value_tail
-
-    pl.semaphore_wait(barrier, len(peers))
-
-    sends = []
-
-    def go(copy):
-        copy.start()
-        sends.append(copy)
-        return copy
-
-    hid_copies = [
-        go(remote(hidden_ref.at[pl.ds(r0, n)], hid.at[h, pl.ds(r0, n)], hsend.at[i], hrecv.at[i], partner))
-        for i, (r0, n) in enumerate(CHUNKS)
-    ]
 
     def kv_lanes(j):
         return pl.ds(j * HD, HD)
@@ -196,8 +196,7 @@
                 )
             )
 
-    for j in range(3):
-        own_blocks(j)
+    own_blocks(0)
     for i in (2, 3, 4, 5):
         loads[i].start()
 
@@ -212,6 +211,8 @@
     sine = jnp.sin(angles)
     sint[...] = jnp.where(even, -sine, sine)
 
+    own_blocks(1)
+
     live = lax.broadcasted_iota(jnp.int32, (BLK, HD), 0) < LIVE
     for i in range(16):
         mask[i * BLK : (i + 1) * BLK, :] = jnp.where(live, 1.0, 0.0).astype(jnp.bfloat16)
@@ -239,22 +240,35 @@
         modded[rows, 0:HALF] = (modv[1:2, 0:HALF] * (a * inv) + modv[0:1, 0:HALF]).astype(jnp.bfloat16)
         modded[rows, HALF:] = (modv[1:2, HALF:] * (b * inv) + modv[0:1, HALF:]).astype(jnp.bfloat16)
 
+    forward_far(0)
+    forward_plane(0)
+    own_blocks(2)
     for i in range(4):
         layer_norm(i)
-    forward_far(0)
-    forward_plane(0)
-
-    mine = pl.ds(pl.multiple_of(c * WIDE + y * PIECE, 16), PIECE)
-    go(
-        remote(
-            wproj_ref.at[mine, lanes_at((1 - h) * HALF, HALF)], wo.at[mine], wsend.at[0], wrecv.at[y], beside
-        )
-    )
-
-    def piece_wait(d):
-        yy = (y + d) % 4
-        ref = wo.at[pl.ds(pl.multiple_of(c * WIDE + yy * PIECE, 16), PIECE)]
-        remote(ref, ref, wsend.at[0], wrecv.at[yy], other).wait_recv()
+
+    def wo_rows(parity, first=0, n=PIECE):
+        return wo.at[pl.ds(pl.multiple_of(c * WIDE + parity * PIECE + first, 16), n)]
+
+    odd = y % 2
+    mine = pl.ds(pl.multiple_of(c * WIDE + odd * PIECE, 16), PIECE)
+    go(remote(wproj_ref.at[mine, lanes_at((1 - h) * HALF, HALF)], wo_rows(odd), wsend.at[0], wrecv.at[0], beside))
+
+    def weight_gather():
+        remote(wo_rows(odd), wo_rows(odd), wsend.at[0], wrecv.at[0], other).wait_recv()
+        for i, dy in enumerate((1, 3)):
+            part = wo_rows(odd, i * 96, 96)
+            go(remote(part, part, wsend.at[1 + i], wrecv.at[1 + i], kv_dev(0, dy, c)))
+        go(remote(wo_rows(odd), wo_rows(odd), wsend.at[3], wrecv.at[3], other))
+
+    def weight_share():
+        for i in range(2):
+            part = wo_rows(1 - odd, i * 96, 96)
+            remote(part, part, wsend.at[0], wrecv.at[1 + i], other).wait_recv()
+        go(remote(wo_rows(1 - odd), wo_rows(1 - odd), wsend.at[4], wrecv.at[4], other))
+
+    def weight_wait():
+        for i in (3, 4):
+            remote(wo_rows(odd), wo_rows(odd), wsend.at[0], wrecv.at[i], other).wait_recv()
 
     def head_out(v, which):
         mean_square = jnp.mean(v * v, axis=1, keepdims=True)
@@ -270,7 +284,18 @@
         pltpu.make_async_copy(qs.at[c * 3 + j], qb.at[j, c], qrecv.at[j, c]).start()
         go(remote(qs.at[(1 - c) * 3 + j], qb.at[j, c], qsend.at[0, j], qrecv.at[j, c], other))
 
-    for part in range(3):
+    loads[2].wait()
+    for j in range(3):
+        pair = jnp.concatenate([w[0, :, j * HD : (j + 1) * HD], w[0, :, WIDE + j * HD : WIDE + (j + 1) * HD]], axis=1)
+        acc = jnp.dot(modded[...], pair, preferred_element_type=jnp.float32)
+        qs[j] = head_out(acc[:, :HD], 0)
+        qs[3 + j] = head_out(acc[:, HD:], 0)
+        if j == 0:
+            send_queries(0)
+    forward_z(0)
+    forward_far(1)
+    forward_plane(1)
+    for part in (1, 2):
         loads[2 + part].wait()
         for g2 in range(3):
             cols = pl.ds(g2 * 256, 256)
@@ -280,15 +305,7 @@
                 continue
             for i in range(2):
                 g = g2 * 2 + i
-                res = head_out(acc[:, i * HD : (i + 1) * HD], part)
-                if part == 1:
-                    fk[0, 0:TOK, g * HD : (g + 1) * HD] = res
-                    continue
-                qs[g] = res
-        if part == 0:
-            send_queries(0)
-            forward_far(1)
-            forward_far(2)
+                fk[0, 0:TOK, g * HD : (g + 1) * HD] = head_out(acc[:, i * HD : (i + 1) * HD], 1)
 
     fresh_row = rows_at(c * (17 * BLK))
     pltpu.make_async_copy(fk.at[:, :, lanes_at(c * WIDE, WIDE)], kvb.at[:, fresh_row, :], fsem.at[c]).start()
@@ -299,10 +316,9 @@
     )
     fresh_out = pltpu.make_async_copy(fk.at[:, pl.ds(0, TOK)], fresh_ref, lsem.at[8])
     fresh_out.start()
+    forward_far(2)
+    forward_plane(2)
     send_queries(1)
-    forward_plane(1)
-    forward_z(0)
-    forward_plane(2)
 
     eye = lax.broadcasted_iota(jnp.int32, (128, 128), 0) == lax.broadcasted_iota(jnp.int32, (128, 128), 1)
 
@@ -415,7 +431,10 @@
         qk(j, r, s2 if i % 2 else s1)
 
     score(0)
+    early = 0
     for i in range(12):
+        if i == 9:
+            early = len(sends)
         if i < 11:
             score(i + 1)
         pv(*units[i], s2 if i % 2 else s1)
@@ -423,16 +442,14 @@
         if i == 0:
             send_queries(2)
             forward_z(1)
-        elif i == 1:
+        elif i == 3:
             forward_z(2)
         elif i == 4:
-            piece_wait(0)
-            for d in (1, 3, 2):
-                go(remote(wo.at[mine], wo.at[mine], wsend.at[d], wrecv.at[y], kv_dev(0, d, c)))
-        elif i == 6:
+            weight_gather()
+        elif i == 7:
             merge(0)
         elif i == 10:
-            merge(1)
+            weight_share()
     def rows_of(weights, j, cols):
         return jnp.concatenate(
             [weights[j * HD : (j + 1) * HD, cols], weights[WIDE + j * HD : WIDE + (j + 1) * HD, cols]], axis=0
@@ -447,16 +464,13 @@
                 acc = term if acc is None else acc + term
             pown[:, cols] = acc
 
-    for d in (1, 3, 2):
-        piece_wait(d)
-    half = wo.at[rows_at(c * WIDE, WIDE)]
-    go(remote(half, half, wsend.at[4], wrecv.at[4], other))
-
     loads[5].wait()
+    merge(1)
     project([(h, wp, 0), (h, wp, 1)], True)
+    for cp in sends[:early]:
+        cp.wait_send()
     merge(2)
-    half = wo.at[rows_at((1 - c) * WIDE, WIDE)]
-    remote(half, half, wsend.at[4], wrecv.at[4], other).wait_recv()
+    weight_wait()
     att_copies[0].wait_recv()
     att_copies[1].wait_recv()
     project([(h, wp, 2), (1 - h, wo, 0), (1 - h, wo, 1)], False)
@@ -471,7 +485,7 @@
         cp.start()
         out_copies.append(cp)
 
-    for cp in sends:
+    for cp in sends[early:]:
         cp.wait_send()
     fresh_out.wait()
     for cp in out_copies:

time: 73.8 us -> 71.6 us (0.970)
  Pallas kernels: 72.1 us -> 70 us
    pallas_call x1, Pallas kernels: 70.1 us -> 68 us  [body(): call(image_hidden, jnp.transpose(mod_table, (1, 0, 2)), step_index, jnp.t...]
where the time goes in v4:
time: 71.6 us; the launch traced here: 71.5 us
  Pallas kernels  70 us (98%)
  between operations  1.47 us (2%)
    pallas_call x1, Pallas kernels, body(): call(image_hidden, jnp.transpose(mod_table, (1, 0, 2)), step_index, jnp.t...  68 us
    pallas_call x1, Pallas kernels, body(): pl.pallas_call(copy_kernel, out_shape=(jax.ShapeDtypeStruct((TOK, HALF),...  2.02 us

profile of v4, /device:TPU:1, one launch (start us, length us, event | category | flops | bytes accessed | tf_op | source)
XLA Modules:
  0.0 71.5 jit_solution(7862440492715196397)
XLA Ops:
  1.3 68.0 %shard_map.113 = (bf16[176,1536]{1,0:T(8,128)(2,1)}, bf16[2,176,768]{2,1,0:T(8,128)(2,1)}) custom-call(bf16[176,1536]{1,0:T(8,128)(2,1)} %hidden_ref.1, f32[3,28,3072]{2,1,0:T(8,128)} %bitcast.4, s32[1]{0:T(128)S(6)} %copy.12.step_ref, bf16[3,3072,768]{2,1,0:T(8,128)(2,1)} %bitcast.3, f32[2,128]{1,0:T(2,128)} %gain_ref.1, bf16[768,3072]{1,0:T(8,128)(2,1)} %wproj_ref.1, ...), custom_call_target="tpu_custom_call" | custom-call | flops 10000000000 | bytes 20000000 | tf_op jit(solution)/shard_map/pallas_call | solution.py:577
  69.3 2.0 %shard_map.114 = (bf16[176,1536]{1,0:T(8,128)(2,1)}, bf16[2,176,768]{2,1,0:T(8,128)(2,1)}) custom-call(bf16[176,1536]{1,0:T(8,128)(2,1)} %get-tuple-element.4.a_ref, bf16[2,176,768]{2,1,0:T(8,128)(2,1)} %get-tuple-element.5.b_ref), custom_call_target="tpu_custom_call" | custom-call | tf_op jit(solution)/shard_map/pallas_call | solution.py:589
